TPU v7x, 512 devices: a whole 4x8x8 slice. The times are simulated.
512 devices in a mesh: hst: 64 (over z, x, core), tensor: 8 (over y).
Axes of the slice: x: 4, y: 8, z: 8, core: 2. Of those that a mesh axis runs over, the one named last changes fastest.
Arguments:
- queries: bfloat16 [12288, 8192], P('hst', 'tensor'), may hold values from -11 to 11
- keys: bfloat16 [12288, 1024], P('hst', 'tensor'), may hold values from -6.5 to 6.5
- values: bfloat16 [12288, 1024], P('hst', 'tensor'), may hold values from -6 to 6
- keep_index: int32 [64, 8, 128], P('hst', 'tensor'), may hold values from 0 to 191, as said below
- keep_count: int32 [64, 8, 1], P('hst', 'tensor'), may hold values from 32 to 96, as said below
Outputs:
- attended: bfloat16 [12288, 8192], P(('hst', 'tensor'))
Inputs may be any that keep to these rules, and one draw needn't show every extreme that they name: `keep_index`: a row within the host block of 192 rows. `keep_count`: slots of a block at or past its count are padding.
All inputs are finite; a program needn't handle non-finite values.
Results may differ from a plain program's by a relative error of at most 0.0065.
Values may be sent and summed in bfloat16 or wider, within the bound.
No kernel may reach another device: no remote copies, remote signals or barrier semaphores. Data moves between devices by JAX's collectives and lax.ppermute only.
A program may use at most 64 MiB of HBM per device.

v0:
```python
import jax
import jax.numpy as jnp
from jax import lax
from jax.sharding import PartitionSpec as P

QH = 64
KVH = 8
HD = 128
ANCHOR = 128
BLOCK = 128


def spread(block, axis, owner):
    block = jnp.where(lax.axis_index(axis) == owner, block, jnp.zeros_like(block))
    return lax.psum(block, axis)


def pick_rows(slot_rows, column):
    return column[slot_rows]


def update(carry, scores, combine, reduce_axes):
    running_max, running_sum, summed = carry
    new_max = jnp.maximum(running_max, jnp.max(scores, axis=reduce_axes))
    rescale = jnp.exp(running_max - new_max)
    expanded = new_max.reshape(new_max.shape + (1,) * len(reduce_axes))
    weights = jnp.exp(scores - expanded)
    running_sum = running_sum * rescale + jnp.sum(weights, axis=reduce_axes)
    summed = summed * rescale[..., None] + combine(weights.astype(jnp.bfloat16))
    return (new_max, running_sum, summed)


def make_fold(query_rows, own_host, live_width, score_scale):

    def fold_hosts(carry, arrived, first_host):
        passed_keys, passed_values, passed_counts = arrived
        host_count = passed_keys.shape[0]
        host_step = max((option for option in (8, 4, 2, 1) if host_count % option == 0))
        slot_total = passed_keys.shape[2]
        slot_place = (lax.broadcasted_iota(jnp.int32, (1, 1, slot_total), 2) % live_width).astype(
            jnp.float32
        )

        def absorb(softmax_state, inputs):
            block_keys, block_values, block_counts, first_source = inputs
            limits = jnp.repeat(block_counts.astype(jnp.float32), live_width, axis=2)
            sources = first_source + lax.broadcasted_iota(jnp.int32, (host_step, 1, 1), 0)
            allowed = (slot_place < limits) & (sources < own_host)
            allowed = jnp.transpose(allowed, (1, 0, 2))[None, :, None]
            scores = (
                jnp.einsum(
                    "ikgd,hknd->ikghn", query_rows, block_keys, preferred_element_type=jnp.float32
                )
                * score_scale
            )
            scores = jnp.where(allowed, scores, -jnp.inf)
            softmax_state = update(
                softmax_state,
                scores,
                lambda weights: jnp.einsum(
                    "ikghn,hknd->ikgd", weights, block_values, preferred_element_type=jnp.float32
                ),
                (3, 4),
            )
            return (softmax_state, None)

        outer_steps = host_count // host_step
        stacked = (
            passed_keys.reshape((outer_steps, host_step) + passed_keys.shape[1:]),
            passed_values.reshape((outer_steps, host_step) + passed_values.shape[1:]),
            passed_counts.reshape((outer_steps, host_step) + passed_counts.shape[1:]),
            host_step * jnp.arange(outer_steps, dtype=jnp.int32),
        )
        carry, ignored = lax.scan(absorb, carry, stacked)
        return carry

    return fold_hosts


def body(queries, keys, values, keep_index, keep_count):
    row_count = queries.shape[0]
    kv_local = keys.shape[1] // HD
    group_size = QH // KVH
    score_scale = HD ** (-0.5)
    own_host = lax.axis_index("hst")
    query_rows = queries.reshape(row_count, kv_local, group_size, HD)
    key_rows = keys.reshape(row_count, kv_local, HD)
    value_rows = values.reshape(row_count, kv_local, HD)
    carry = (
        jnp.full((row_count, kv_local, group_size), -jnp.inf, jnp.float32),
        jnp.zeros((row_count, kv_local, group_size), jnp.float32),
        jnp.zeros((row_count, kv_local, group_size, HD), jnp.float32),
    )
    local_scores = (
        jnp.einsum("ikgd,jkd->ikgj", query_rows, key_rows, preferred_element_type=jnp.float32)
        * score_scale
    )
    causal = lax.broadcasted_iota(
        jnp.int32, (row_count, 1, 1, row_count), 0
    ) >= lax.broadcasted_iota(jnp.int32, (row_count, 1, 1, row_count), 3)
    local_scores = jnp.where(causal, local_scores, -jnp.inf)
    carry = update(
        carry,
        local_scores,
        lambda weights: jnp.einsum(
            "ikgj,jkd->ikgd", weights, value_rows, preferred_element_type=jnp.float32
        ),
        (3,),
    )
    anchor_keys, anchor_values = (
        spread(key_rows[:ANCHOR], "hst", 0),
        spread(value_rows[:ANCHOR], "hst", 0),
    )
    anchor_scores = (
        jnp.einsum("ikgd,jkd->ikgj", query_rows, anchor_keys, preferred_element_type=jnp.float32)
        * score_scale
    )
    anchor_scores = jnp.where(own_host > 0, anchor_scores, -jnp.inf)
    carry = update(
        carry,
        anchor_scores,
        lambda weights: jnp.einsum(
            "ikgj,jkd->ikgd", weights, anchor_values, preferred_element_type=jnp.float32
        ),
        (3,),
    )
    picker = jax.vmap(pick_rows, in_axes=(0, 1))
    counts_sent = keep_count.astype(jnp.bfloat16)
    slot_rows = keep_index[0]
    fold_hosts = make_fold(query_rows, own_host, BLOCK, score_scale)
    carry = fold_hosts(
        carry,
        (
            lax.all_gather(picker(slot_rows, key_rows)[None], "hst", axis=0, tiled=True),
            lax.all_gather(picker(slot_rows, value_rows)[None], "hst", axis=0, tiled=True),
            lax.all_gather(counts_sent, "hst", axis=0, tiled=True),
        ),
        jnp.int32(0),
    )
    running_max, running_sum, summed = carry
    attended = (summed / running_sum[..., None]).astype(jnp.bfloat16).reshape(row_count, -1)
    return lax.all_to_all(attended, "tensor", split_axis=0, concat_axis=1, tiled=True)


def solution(mesh):
    placed = (
        P("hst", "tensor"),
        P("hst", "tensor"),
        P("hst", "tensor"),
        P("hst", "tensor", None),
        P("hst", "tensor", None),
    )
    return jax.shard_map(
        body, mesh=mesh, in_specs=placed, out_specs=P(("hst", "tensor"), None), check_vma=False
    )
```

profile of v0, /device:TPU:1, one launch (start us, length us, event | category | flops | bytes accessed | tf_op | source)
XLA Modules:
  0.0 456.2 jit_solution(15936242338143684338)
XLA Ops:
  6.5 1.4 slice_select_fusion
  8.0 1.4 slice_select_fusion.1
  10.0 1.3 dynamic-slice
  11.3 0.7 dynamic-update-slice
  12.7 0.7 compare_select_fusion
  13.4 2.3 gather_fusion
  15.8 2.4 gather_fusion.1
  18.2 1.4 fusion.55
  19.9 0.7 copy.34
  20.8 177.9 %all-reduce.4.cloned.1.call-done = (bf16[128,128]{1,0:T(8,128)(2,1)}, bf16[128,128]{1,0:T(8,128)(2,1)}, bf16[64]{0:T(256)(128)(2,1)}) async-done(((bf16[128,128]{1,0:T(8,128)(2,1)}, bf16[128,128]{1,0:T(8,128)(2,1)}, bf16[64]{0:T(256)(128)(2,1)}), (bf16[128,128]{1,0:T(8,128)(2,1)}, bf16[128,128]{1,0:T(8,128)(2,1)}, bf16[64]{0:T(256)(128)(2,1)})) %all-reduce.4.cloned.1.call-update) | async-done | bytes 65680 | tf_op jit(solution)/shard_map/psum | solution.py:15
  198.6 1.3 fusion.56
  201.4 1.1 fusion.33
  202.8 79.4 %all-gather.5.cloned.1.call-done = bf16[8192,128]{1,0:T(8,128)(2,1)} async-done(((bf16[128,128]{1,0:T(8,128)(2,1)}), bf16[8192,128]{1,0:T(8,128)(2,1)}) %all-gather.5.cloned.1.call-update) | async-done | bytes 2097168 | tf_op jit(solution)/shard_map/all_gather | solution.py:134
  282.2 84.0 %all-gather.7.cloned.1.call-done = bf16[8192,128]{1,0:T(8,128)(2,1)} async-done(((bf16[128,128]{1,0:T(8,128)(2,1)}), bf16[8192,128]{1,0:T(8,128)(2,1)}) %all-gather.7.cloned.1.call-update) | async-done | bytes 2097168 | tf_op jit(solution)/shard_map/all_gather | solution.py:135
  366.2 61.5 %while.15 = (s32[]{:T(128)}, f32[192,1,8]{0,2,1:T(8,128)S(1)}, f32[192,1,8]{0,2,1:T(8,128)S(1)}, f32[192,1,8,128]{3,0,2,1:T(8,128)S(1)}, bf16[8,8,1,1]{1,3,2,0:T...) while((s32[]{:T(128)}, f32[192,1,8]{0,2,1:T(8,128)S(1)}, ...), condition=%wide.region_9.10_spmd.clone, body=%wide.region_6.9_spmd.clone.sunk | while | flops 823008640 | bytes 21469412 | solution.py:74
  366.7 0.7 add_compare_fusion.2
  367.5 2.0 bitcast_reduce_fusion.2
  369.5 2.7 fusion.73
  372.3 1.6 fusion.72
  374.4 0.7 add_compare_fusion.2
  375.2 2.0 bitcast_reduce_fusion.2
  377.2 2.7 fusion.73
  379.9 1.6 fusion.72
  382.1 0.7 add_compare_fusion.2
  382.9 2.0 bitcast_reduce_fusion.2
  384.9 2.7 fusion.73
  387.6 1.6 fusion.72
  389.8 0.7 add_compare_fusion.2
  390.6 2.0 bitcast_reduce_fusion.2
  392.6 2.7 fusion.73
  395.3 1.6 fusion.72
  397.5 0.7 add_compare_fusion.2
  398.3 2.0 bitcast_reduce_fusion.2
  400.3 2.7 fusion.73
  403.0 1.6 fusion.72
  405.2 0.7 add_compare_fusion.2
  406.0 2.0 bitcast_reduce_fusion.2
  408.0 2.7 fusion.73
  410.7 1.6 fusion.72
  412.9 0.7 add_compare_fusion.2
  413.6 2.0 bitcast_reduce_fusion.2
  415.7 2.7 fusion.73
  418.4 1.6 fusion.72
  421.3 2.0 bitcast_reduce_fusion.2
  423.4 2.7 fusion.73
  426.1 1.6 fusion.72
  428.4 20.5 %all_to_all.19 = bf16[8,24,1024]{2,1,0:T(8,128)(2,1)S(1)} all-to-all(bf16[8,24,1024]{2,1,0:T(8,128)(2,1)S(1)} %all_to_all.14), channel_id=1, replica_groups=mesh['hst'=64,'tensor'=8] {'tensor'}, dimensions={0} | all-to-all | bytes 786432 | tf_op jit(solution)/shard_map/all_to_all | solution.py:142
  448.9 0.8 copy.49
  (90 shorter events, 9.9 us)
Async XLA Ops:
  6.5 194.3 %copy-start.1 = (bf16[192,128]{1,0:T(8,128)(2,1)S(1)}, bf16[192,128]{1,0:T(8,128)(2,1)}, u32[]{:S(2)}) copy-start(bf16[192,128]{1,0:T(8,128)(2,1)} %param.9) | copy-start | bytes 147460
  6.5 14.1 %copy-start = (bf16[192,1024]{1,0:T(8,128)(2,1)S(1)}, bf16[192,1024]{1,0:T(8,128)(2,1)}, u32[]{:S(2)}) copy-start(bf16[192,1024]{1,0:T(8,128)(2,1)} %param.7) | copy-start | bytes 1179652
  6.5 192.1 %all-reduce.4.cloned.1.call-start = ((), (), s32[]{:S(2)}) async-start(), calls=%async_computation.3 | async-start | bytes 132096 | tf_op jit(solution)/shard_map/psum | solution.py:15
  12.0 0.6 copy-start.2
  12.6 269.6 %all-gather.5.cloned.1.call-start = ((), (), s32[]{:S(2)}) async-start(), calls=%async_computation.1 | async-start | bytes 2129920 | tf_op jit(solution)/shard_map/all_gather | solution.py:134
  15.7 350.4 %all-gather.7.cloned.1.call-start = ((), (), s32[]{:S(2)}) async-start(), calls=%async_computation.2 | async-start | bytes 2129920 | tf_op jit(solution)/shard_map/all_gather | solution.py:135
  198.6 4.1 copy-start.3
Sparse Core Ops, SparseCore 0:
  12.7 185.8 all-reduce.3
  202.0 80.1 all-gather.4
  285.5 80.5 all-gather.6
where the time goes:
time: 457 us; the launch traced here: 456 us
  waiting for transfers between devices  341 us (75%)
  matrix products  42.2 us (9%)
  other arithmetic  23.2 us (5%)
  blocking collectives  20.5 us (4%)
  local copies, waits for them, and re-layouts  14.5 us (3%)
  between operations  13.9 us (3%)
    psum x1, waiting for transfers between devices, spread(): return lax.psum(block, axis)  178 us
    all_gather x1, waiting for transfers between devices, body(): lax.all_gather(picker(slot_rows, value_rows)[None], 'hst', axis=0, tiled=...  84 us
    all_gather x1, waiting for transfers between devices, body(): lax.all_gather(picker(slot_rows, key_rows)[None], 'hst', axis=0, tiled=True)  79.4 us
    dot_general x8, matrix products, absorb(): jnp.einsum('ikghn,hknd->ikgd', weights, block_values, preferred_element_t...  21.6 us
    all_to_all x1, blocking collectives, body(): lax.all_to_all(attended, 'tensor', split_axis=0, concat_axis=1, tiled=True)  20.5 us
    dot_general x8, matrix products, absorb(): jnp.einsum('ikgd,hknd->ikghn', query_rows, block_keys, preferred_element_...  16.2 us
    reduce_sum x8, other arithmetic, update(): running_sum = running_sum * rescale + jnp.sum(weights, axis=reduce_axes)  12.4 us
  transfers between devices with their start and end apart: 3, of which 3 were waited for; matrix products, arithmetic and copies ran while one was open for 3% of the time, Pallas kernels for 0%

commit v1 on v0

v1 whole, which is shorter than its diff:
```python
import jax
import jax.numpy as jnp
from jax import lax
from jax.experimental import pallas as pl
from jax.experimental.pallas import tpu as pltpu
from jax.sharding import Mesh, PartitionSpec as P

QH = 64
KVH = 8
HD = 128
TOK = 192
ANCHOR = 128
GROUP = QH // KVH
ROWS = GROUP * TOK
LIVE = 96
MARK = 16.0
LIMIT = 8.0
Z, X, C, T = 8, 4, 2, 8
HALF = ANCHOR
SLOT = 2 * LIVE + HALF
LIST = Z * LIVE
COLUMN = 2 * LIST + HALF
TILE = 384
NEG = -1e30
LOG2E = 1.4426950408889634
SCALE = HD ** (-0.5) * LOG2E
LIMIT_BYTES = 40 * 1024 * 1024

VM = pl.BlockSpec(memory_space=pltpu.VMEM)
SM = pl.BlockSpec(memory_space=pltpu.SMEM)


def call(kernel, out_shape, in_specs, out_specs, scratch=(), flops=0):
    return pl.pallas_call(
        kernel,
        out_shape=out_shape,
        in_specs=in_specs,
        out_specs=out_specs,
        scratch_shapes=list(scratch),
        compiler_params=pltpu.CompilerParams(vmem_limit_bytes=LIMIT_BYTES),
        cost_estimate=pl.CostEstimate(flops=flops, bytes_accessed=1 << 20, transcendentals=0),
    )


def pick_kernel(count_ref, index_ref, keys_ref, values_ref, out_ref):
    count = count_ref[0, 0, 0]
    index = index_ref[0]
    lane = lax.broadcasted_iota(jnp.int32, (1, HD), 1)
    first = jnp.sum(jnp.where(lane == 0, index, 0))
    index = jnp.where(lane < count, index, first)
    row = lax.broadcasted_iota(jnp.int32, (TOK, HD), 0)
    hot = (row == index).astype(jnp.float32).astype(jnp.bfloat16)
    contract = (((0,), (0,)), ((), ()))
    picked_keys = lax.dot_general(hot, keys_ref[...], contract, preferred_element_type=jnp.float32)
    picked_values = lax.dot_general(
        hot, values_ref[...], contract, preferred_element_type=jnp.float32
    )
    slot = lax.broadcasted_iota(jnp.int32, (HD, HD), 0)
    picked_values = jnp.where(slot < count, picked_values, MARK)
    out_ref[:LIVE] = picked_keys[:LIVE].astype(jnp.bfloat16)
    out_ref[LIVE:] = picked_values[:LIVE].astype(jnp.bfloat16)


def spread_kernel(place_ref, picked_ref, keys_ref, passed_ref, out_ref):
    even = place_ref[1] == 0
    half = jnp.where(even, keys_ref[:ANCHOR].astype(jnp.float32), passed_ref[...].astype(jnp.float32))
    half = half.astype(jnp.bfloat16)
    for to in range(Z):
        out_ref[to, : 2 * LIVE] = picked_ref[...]
        out_ref[to, 2 * LIVE :] = half


def regroup_kernel(blocks_ref, out_ref):
    for to in range(X):
        for z in range(Z):
            out_ref[to, z * LIVE : (z + 1) * LIVE] = blocks_ref[z, :LIVE]
            out_ref[to, LIST + z * LIVE : LIST + (z + 1) * LIVE] = blocks_ref[z, LIVE : 2 * LIVE]
        out_ref[to, 2 * LIST :] = blocks_ref[0, 2 * LIVE :]


def fold(tile, queries_ref, key_rows, value_rows, most_ref, total_ref, mask=None, first=False):
    at = pl.ds(tile * TILE, TILE)
    scores = lax.dot_general(
        queries_ref[at, :],
        key_rows,
        (((1,), (1,)), ((), ())),
        preferred_element_type=jnp.float32,
    )
    if mask is not None:
        scores = jnp.where(mask, scores, NEG)
    peak = jnp.max(scores, axis=1, keepdims=True)
    if first:
        most = jnp.broadcast_to(peak, (TILE, HD))
    else:
        before = most_ref[at, :]
        most = jnp.maximum(before, peak)
    weights = jnp.exp2((scores - most[:, :1]) * SCALE).astype(jnp.bfloat16)
    added = jnp.dot(weights, value_rows, preferred_element_type=jnp.float32)
    if first:
        total_ref[at, :] = added
    else:
        ratio = jnp.exp2((before - most) * SCALE)
        total_ref[at, :] = total_ref[at, :] * jnp.concatenate([ratio, ratio], axis=1) + added
    most_ref[at, :] = most


def fill(stacked, queries_ref):
    for head in range(GROUP):
        stacked[head * TOK : (head + 1) * TOK, :] = queries_ref[:, head * HD : (head + 1) * HD]


def marked(values, keep):
    ok = (values < LIMIT) & keep
    kept = jnp.where(ok, values, 0.0).astype(jnp.bfloat16)
    ones = jnp.where(ok, 1.0, 0.0).astype(jnp.bfloat16)
    return jnp.concatenate([kept, ones], axis=1)


def columns(place_ref, core, stand_in, columns_ref, stacked, most_ref, total_ref):
    own_z, own_side = place_ref[0], place_ref[2] * C + place_ref[1]
    row = lax.broadcasted_iota(jnp.int32, (LIST, HD), 0)

    def column(x, carry):
        hosts = own_z + (x * C + core < own_side).astype(jnp.int32)
        keep = row < hosts * LIVE
        key_rows = columns_ref[x, :LIST].astype(jnp.float32)
        key_rows = jnp.where(keep, key_rows, stand_in).astype(jnp.bfloat16)
        value_rows = marked(columns_ref[x, LIST : 2 * LIST].astype(jnp.float32), keep)
        for tile in range(ROWS // TILE):
            fold(tile, stacked, key_rows, value_rows, most_ref, total_ref)
        return carry

    lax.fori_loop(0, X, column, 0)


def near_kernel(place_ref, queries_ref, keys_ref, values_ref, columns_ref, most_ref, total_ref, stacked):
    fill(stacked, queries_ref)
    row = lax.broadcasted_iota(jnp.int32, (TILE, TOK), 0)
    token = jnp.where(row >= TOK, row - TOK, row)
    causal = token >= lax.broadcasted_iota(jnp.int32, (TILE, TOK), 1)
    value_rows = jnp.concatenate([values_ref[...], jnp.ones((TOK, HD), jnp.bfloat16)], axis=1)
    for tile in range(ROWS // TILE):
        fold(tile, stacked, keys_ref[...], value_rows, most_ref, total_ref, causal, True)
    stand_in = keys_ref[:1].astype(jnp.float32)
    columns(place_ref, place_ref[1], stand_in, columns_ref, stacked, most_ref, total_ref)


def far_kernel(
    place_ref, queries_ref, keys_ref, own_half_ref, columns_ref, most_in, total_in, out_ref, stacked, most_ref, total_ref
):
    fill(stacked, queries_ref)
    stand_in = keys_ref[:1].astype(jnp.float32)
    most_ref[...] = most_in[...]
    total_ref[...] = total_in[...]
    columns(place_ref, 1 - place_ref[1], stand_in, columns_ref, stacked, most_ref, total_ref)
    even = place_ref[1] == 0
    mine = own_half_ref[...].astype(jnp.float32)
    other = columns_ref[0, 2 * LIST :].astype(jnp.float32)
    row = lax.broadcasted_iota(jnp.int32, (ANCHOR, HD), 0)
    own = place_ref[0] * (X * C) + place_ref[2] * C + place_ref[1]
    keep = row < jnp.where(own > 0, ANCHOR, 0)
    key_rows = jnp.where(keep, jnp.where(even, mine, other), stand_in).astype(jnp.bfloat16)
    value_rows = marked(jnp.where(even, other, mine), keep)
    for tile in range(ROWS // TILE):
        fold(tile, stacked, key_rows, value_rows, most_ref, total_ref)
    for head in range(GROUP):
        at = pl.ds(head * TOK, TOK)
        done = total_ref[at, :HD] / total_ref[at, HD:]
        out_ref[:, head * HD : (head + 1) * HD] = done.astype(jnp.bfloat16)


def body(queries, keys, values, keep_index, keep_count):
    half = jnp.bfloat16
    place = jnp.stack(
        [lax.axis_index("z"), lax.axis_index("core"), lax.axis_index("x"), lax.axis_index("x")]
    ).astype(jnp.int32)
    passed = lax.ppermute(values[:ANCHOR], ("z", "x", "core"), [(0, 1)])
    picked = call(
        pick_kernel, jax.ShapeDtypeStruct((2 * LIVE, HD), half), [SM, VM, VM, VM], VM, flops=1 << 24
    )(keep_count, keep_index, keys, values)
    blocks = call(
        spread_kernel, jax.ShapeDtypeStruct((Z, SLOT, HD), half), [SM, VM, VM, VM], VM
    )(place, picked, keys, passed)
    blocks = lax.all_to_all(blocks, "z", 0, 0, tiled=True)
    column = call(
        regroup_kernel, jax.ShapeDtypeStruct((X, COLUMN, HD), half), [VM], VM
    )(blocks)
    column = lax.all_to_all(column, "x", 0, 0, tiled=True)
    other = lax.ppermute(column, "core", [(0, 1), (1, 0)])
    flops = 4 * ROWS * X * LIST * HD
    most, total = call(
        near_kernel,
        (
            jax.ShapeDtypeStruct((ROWS, HD), jnp.float32),
            jax.ShapeDtypeStruct((ROWS, 2 * HD), jnp.float32),
        ),
        [SM, VM, VM, VM, VM],
        (VM, VM),
        [pltpu.VMEM((ROWS, HD), half)],
        flops,
    )(place, queries, keys, values, column)
    attended = call(
        far_kernel,
        jax.ShapeDtypeStruct((TOK, GROUP * HD), half),
        [SM, VM, VM, VM, VM, VM, VM],
        VM,
        [
            pltpu.VMEM((ROWS, HD), half),
            pltpu.VMEM((ROWS, HD), jnp.float32),
            pltpu.VMEM((ROWS, 2 * HD), jnp.float32),
        ],
        flops,
    )(place, queries, keys, column[0, 2 * LIST :], other, most, total)
    return lax.all_to_all(attended, "tensor", split_axis=0, concat_axis=1, tiled=True)


def solution(mesh):
    parts = Mesh(mesh.devices.reshape(Z, X, C, T), ("z", "x", "core", "tensor"))
    hosts = ("z", "x", "core")
    placed = (
        P(hosts, "tensor"),
        P(hosts, "tensor"),
        P(hosts, "tensor"),
        P(hosts, "tensor", None),
        P(hosts, "tensor", None),
    )
    return jax.shard_map(
        body, mesh=parts, in_specs=placed, out_specs=P(hosts + ("tensor",), None), check_vma=False
    )
```

time: 457 us -> 110 us (0.24)
  waiting for transfers between devices: 341 us -> 4.23 us
  blocking collectives: 20.5 us -> 70.5 us
  matrix products: 42.2 us -> 0 us
  other arithmetic: 23.2 us -> 0.08 us
  Pallas kernels: 0 us -> 23.1 us
  between operations: 13.9 us -> 0.79 us
  local copies, waits for them, and re-layouts: 14.5 us -> 4.6 us
  starting transfers between devices: 0.09 us -> 6.48 us
    psum x1 -> x0, waiting for transfers between devices: 178 us -> none  [spread(): return lax.psum(block, axis)]
    all_gather x2 -> x0, waiting for transfers between devices: 163 us -> none  [the longest x1 84 us: body(): lax.all_gather(picker(slot_rows, value_rows)[None], 'hst', axis=0, tiled=...]
    all_to_all x0 -> x2, blocking collectives: none -> 48.7 us  [the longest x1 25 us: body(): blocks = lax.all_to_all(blocks, 'z', 0, 0, tiled=True)]
    dot_general x20 -> x0, matrix products: 42.2 us -> none  [the longest x8 21.6 us: absorb(): jnp.einsum('ikghn,hknd->ikgd', weights, block_values, preferred_element_t...]
    pallas_call x0 -> x5, Pallas kernels: none -> 23.1 us  [the longest x1 11.1 us: body(): call(far_kernel, jax.ShapeDtypeStruct((TOK, GROUP * HD), half), [SM, VM,...]
    reduce_sum x8 -> x0, other arithmetic: 12.4 us -> none  [update(): running_sum = running_sum * rescale + jnp.sum(weights, axis=reduce_axes)]
    ppermute x0 -> x2, starting transfers between devices: none -> 6.48 us  [the longest x1 5.2 us: body(): other = lax.ppermute(column, 'core', [(0, 1), (1, 0)])]
    lt x16 -> x0, other arithmetic: 5.24 us -> none  [absorb(): allowed = (slot_place < limits) & (sources < own_host)]
  transfers between devices with their start and end apart: 3 -> 2, of which waited for: 3 -> 1; matrix products, arithmetic and copies ran while one was open for 3% -> 0% of each run, Pallas kernels for 0% -> 10%
where the time goes in v1:
time: 110 us
  blocking collectives  70.5 us (64%)
  Pallas kernels  23.1 us (21%)
  starting transfers between devices  6.48 us (6%)
  local copies, waits for them, and re-layouts  4.6 us (4%)
  waiting for transfers between devices  4.23 us (4%)
    all_to_all x1, blocking collectives, body(): blocks = lax.all_to_all(blocks, 'z', 0, 0, tiled=True)  25 us
    all_to_all x1, blocking collectives, body(): column = lax.all_to_all(column, 'x', 0, 0, tiled=True)  23.7 us
    all_to_all x1, blocking collectives, body(): lax.all_to_all(attended, 'tensor', split_axis=0, concat_axis=1, tiled=True)  21.8 us
    pallas_call x1, Pallas kernels, body(): call(far_kernel, jax.ShapeDtypeStruct((TOK, GROUP * HD), half), [SM, VM,...  11.1 us
    pallas_call x1, Pallas kernels, body(): call(near_kernel, (jax.ShapeDtypeStruct((ROWS, HD), jnp.float32), jax.Sha...  10.8 us
    ppermute x1, starting transfers between devices, body(): other = lax.ppermute(column, 'core', [(0, 1), (1, 0)])  5.2 us
    ppermute x1, waiting for transfers between devices, body(): passed = lax.ppermute(values[:ANCHOR], ('z', 'x', 'core'), [(0, 1)])  4.22 us
    unnamed x14, local copies, waits for them, and re-layouts  3.06 us
  transfers between devices with their start and end apart: 2, of which 1 were waited for; matrix products, arithmetic and copies ran while one was open for 0% of the time, Pallas kernels for 10%

profile of v1, /device:TPU:1, one launch (start us, length us, event | category | flops | bytes accessed | tf_op | source)
XLA Modules:
  0.0 109.7 jit_solution(17161527837753801184)
XLA Ops:
  0.0 0.8 slice.6
  0.8 1.3 %collective-permute-start = (bf16[128,128]{1,0:T(8,128)(2,1)S(1)}, bf16[128,128]{1,0:T(8,128)(2,1)S(1)}, u32[]{:S(2)}, u32[]{:S(2)}) collective-permute-start(bf16[128,128]{1,0:T(8,128)(2,1)S(1)} %slice.6), channel_id=1, source_target_pairs={{0,8},{1,9},{2,10},{3,11},{4,12},{5,13},{6,14},{7,15}} | collective-permute-start | bytes 98312 | tf_op jit(solution)/shard_map/ppermute | solution.py:177
  2.1 0.1 pad_add_fusion.place_ref
  2.8 0.0 copy-start
  2.8 0.8 copy-done
  3.6 0.0 copy-start.3
  3.6 0.8 copy-done.3
  4.4 0.0 copy-start.5
  4.4 0.7 copy-done.5
  5.0 0.3 shard_map.55.picked_ref
  5.4 4.2 %collective-permute-done.passed_ref = bf16[128,128]{1,0:T(8,128)(2,1)S(1)} collective-permute-done((bf16[128,128]{1,0:T(8,128)(2,1)S(1)}, bf16[128,128]{1,0:T(8,128)(2,1)S(1)}, u32[]{:S(2)}, u32[]{:S(2)}) %collective-permute-start) | collective-permute-done | bytes 32800 | tf_op jit(solution)/shard_map/ppermute | solution.py:177
  9.6 0.0 copy-start.1
  9.6 0.8 copy-done.1
  10.4 0.6 shard_map.56
  11.0 25.0 %all_to_all.29.blocks_ref = bf16[8,320,128]{2,1,0:T(8,128)(2,1)S(1)} all-to-all(bf16[8,320,128]{2,1,0:T(8,128)(2,1)S(1)} %shard_map.56), channel_id=1, replica_groups=mesh['z'=8,'x'=4,'core'=2,'tensor'=8] {'z'}, dimensions={0} | all-to-all | bytes 1310720 | tf_op jit(solution)/shard_map/all_to_all | solution.py:184
  36.0 0.2 shard_map.57
  36.2 0.0 copy-start.2
  36.2 0.0 copy-start.4
  36.2 0.0 copy-start.6
  36.3 23.7 %all_to_all.30.columns_ref = bf16[4,1664,128]{2,1,0:T(8,128)(2,1)S(1)} all-to-all(bf16[4,1664,128]{2,1,0:T(8,128)(2,1)S(1)} %shard_map.57), channel_id=1, replica_groups=mesh['z'=8,'x'=4,'core'=2,'tensor'=8] {'x'}, dimensions={0} | all-to-all | bytes 3407872 | tf_op jit(solution)/shard_map/all_to_all | solution.py:188
  60.0 5.2 %collective-permute-start.1 = (bf16[4,1664,128]{2,1,0:T(8,128)(2,1)S(1)}, bf16[4,1664,128]{2,1,0:T(8,128)(2,1)S(1)}, u32[]{:S(2)}, u32[]{:S(2)}) collective-permute-start(bf16[4,1664,128]{2,1,0:T(8,128)(2,1)S(1)} %all_to_all.30.columns_ref), channel_id=1, source_target_pairs={{0,8},{8,0},{1,9},{9,1},{2,10},{10,2},{3,11},{11,3},{4,12},{12,4},... | collective-permute-start | bytes 5111816 | tf_op jit(solution)/shard_map/ppermute | solution.py:189
  65.2 0.0 copy-done.2
  65.2 0.0 copy-done.4
  65.2 0.0 copy-done.6
  65.2 10.8 %shard_map.58 = (f32[1536,128]{1,0:T(8,128)S(1)}, f32[1536,256]{1,0:T(8,128)S(1)}) custom-call(s32[4]{0:T(128)S(1)} %pad_add_fusion.place_ref, bf16[192,1024]{1,0:T(8,128)(2,1)S(1)} %copy-done.6, bf16[192,128]{1,0:T(8,128)(2,1)S(1)} %copy-done.2, bf16[192,128]{1,0:T(8,128)(2,1)S(1)} %copy-done.4, bf16[4,1664,128]{2,1,0:T(8,128)(2,1)S(1)} %all_to_all.30.columns_ref), custom_call_target="tpu_custom_call" | custom-call | flops 2415919104 | bytes 1048576 | tf_op jit(solution)/shard_map/pallas_call | solution.py:191
  76.0 0.0 collective-permute-done.1.columns_ref
  76.0 11.1 %shard_map.59 = bf16[192,1024]{1,0:T(8,128)(2,1)S(1)} custom-call(s32[4]{0:T(128)S(1)} %pad_add_fusion.place_ref, bf16[192,1024]{1,0:T(8,128)(2,1)S(1)} %copy-done.6, bf16[192,128]{1,0:T(8,128)(2,1)S(1)} %copy-done.2, bf16[128,128]{1,0:T(8,128)(2,1)S(1)} %slice_bitcast_fusion.own_half_ref, bf16[4,1664,128]{2,1,0:T(8,128)(2,1)S(1)} %collective-permute-done.1.columns_ref, ...), custom_call_target="tpu_custom_call" | custom-call | flops 2415919104 | bytes 1048576 | tf_op jit(solution)/shard_map/pallas_call | solution.py:202
  87.2 21.8 %all_to_all.31 = bf16[8,24,1024]{2,1,0:T(8,128)(2,1)S(1)} all-to-all(bf16[8,24,1024]{2,1,0:T(8,128)(2,1)S(1)} %bitcast.9), channel_id=1, replica_groups=mesh['z'=8,'x'=4,'core'=2,'tensor'=8] {'tensor'}, dimensions={0} | all-to-all | bytes 786432 | tf_op jit(solution)/shard_map/all_to_all | solution.py:214
  109.0 0.8 copy.7
  (1 shorter events, 0.0 us)
Async XLA Ops:
  0.8 8.8 %collective-permute-start = (bf16[128,128]{1,0:T(8,128)(2,1)S(1)}, bf16[128,128]{1,0:T(8,128)(2,1)S(1)}, u32[]{:S(2)}, u32[]{:S(2)}) collective-permute-start(bf16[128,128]{1,0:T(8,128)(2,1)S(1)} %slice.6), channel_id=1, source_target_pairs={{0,8},{1,9},{2,10},{3,11},{4,12},{5,13},{6,14},{7,15}} | collective-permute-start | bytes 98312 | tf_op jit(solution)/shard_map/ppermute | solution.py:177
  2.8 0.8 copy-start
  3.6 0.8 copy-start.3
  4.4 0.7 copy-start.5
  9.6 0.8 copy-start.1
  36.2 29.0 %copy-start.2 = (bf16[192,128]{1,0:T(8,128)(2,1)S(1)}, bf16[192,128]{1,0:T(8,128)(2,1)}, u32[]{:S(2)}) copy-start(bf16[192,128]{1,0:T(8,128)(2,1)} %keys_ref.7) | copy-start | bytes 147460
  36.2 29.0 %copy-start.4 = (bf16[192,128]{1,0:T(8,128)(2,1)S(1)}, bf16[192,128]{1,0:T(8,128)(2,1)}, u32[]{:S(2)}) copy-start(bf16[192,128]{1,0:T(8,128)(2,1)} %values_ref.3) | copy-start | bytes 147460
  36.2 29.0 %copy-start.6 = (bf16[192,1024]{1,0:T(8,128)(2,1)S(1)}, bf16[192,1024]{1,0:T(8,128)(2,1)}, u32[]{:S(2)}) copy-start(bf16[192,1024]{1,0:T(8,128)(2,1)} %queries_ref.3) | copy-start | bytes 1179652
  60.0 16.0 %collective-permute-start.1 = (bf16[4,1664,128]{2,1,0:T(8,128)(2,1)S(1)}, bf16[4,1664,128]{2,1,0:T(8,128)(2,1)S(1)}, u32[]{:S(2)}, u32[]{:S(2)}) collective-permute-start(bf16[4,1664,128]{2,1,0:T(8,128)(2,1)S(1)} %all_to_all.30.columns_ref), channel_id=1, source_target_pairs={{0,8},{8,0},{1,9},{9,1},{2,10},{10,2},{3,11},{11,3},{4,12},{12,4},... | collective-permute-start | bytes 5111816 | tf_op jit(solution)/shard_map/ppermute | solution.py:189

commit v2 on v1

v2 whole, which is shorter than its diff:
```python
import jax
import jax.numpy as jnp
from jax import lax
from jax.experimental import pallas as pl
from jax.experimental.pallas import tpu as pltpu
from jax.sharding import Mesh, PartitionSpec as P

QH = 64
KVH = 8
HD = 128
TOK = 192
ANCHOR = 128
GROUP = QH // KVH
ROWS = GROUP * TOK
LIVE = 96
MARK = 16.0
LIMIT = 8.0
Z, X, C, T = 8, 4, 2, 8
HALF = ANCHOR
SLOT = 2 * LIVE + HALF
LIST = Z * LIVE
COLUMN = 2 * LIST + HALF
PIECE = 16
TILE = 768
ONES = 8
SAFE = 2.0**100
NEG = -1e30
LOG2E = 1.4426950408889634
SCALE = HD ** (-0.5) * LOG2E
LIMIT_BYTES = 40 * 1024 * 1024

VM = pl.BlockSpec(memory_space=pltpu.VMEM)
HBM = pl.BlockSpec(memory_space=pltpu.HBM)


def call(kernel, out_shape, in_specs, out_specs, scratch=(), flops=0, limit=LIMIT_BYTES):
    return pl.pallas_call(
        kernel,
        out_shape=out_shape,
        in_specs=in_specs,
        out_specs=out_specs,
        scratch_shapes=list(scratch),
        compiler_params=pltpu.CompilerParams(vmem_limit_bytes=limit),
        cost_estimate=pl.CostEstimate(flops=flops, bytes_accessed=1 << 20, transcendentals=0),
    )


def pack_kernel(
    count_in, index_in, keys_in, values_in, passed_ref, out_ref, count_ref, index_ref, keys_ref, values_ref, sems
):
    pairs = (
        (count_in, count_ref),
        (index_in, index_ref),
        (keys_in, keys_ref),
        (values_in, values_ref),
    )
    copies = [pltpu.make_async_copy(a, b, sems.at[n]) for n, (a, b) in enumerate(pairs)]
    for copy in copies:
        copy.start()
    for copy in copies:
        copy.wait()
    count = count_ref[0, 0, 0]
    index = index_ref[0]
    lane = lax.broadcasted_iota(jnp.int32, (1, HD), 1)
    first = jnp.sum(jnp.where(lane == 0, index, 0))
    index = jnp.where(lane < count, index, first)
    row = lax.broadcasted_iota(jnp.int32, (TOK, HD), 0)
    hot = (row == index).astype(jnp.float32).astype(jnp.bfloat16)
    contract = (((0,), (0,)), ((), ()))
    picked_keys = lax.dot_general(hot, keys_ref[...], contract, preferred_element_type=jnp.float32)
    picked_values = lax.dot_general(
        hot, values_ref[...], contract, preferred_element_type=jnp.float32
    )
    slot = lax.broadcasted_iota(jnp.int32, (HD, HD), 0)
    picked_values = jnp.where(slot < count, picked_values, MARK)
    even = lax.axis_index("core") == 0
    half = jnp.where(even, keys_ref[:ANCHOR].astype(jnp.float32), passed_ref[:ANCHOR].astype(jnp.float32))
    half = half.astype(jnp.bfloat16)
    for to in range(Z):
        out_ref[to, :LIVE] = picked_keys[:LIVE].astype(jnp.bfloat16)
        out_ref[to, LIVE : 2 * LIVE] = picked_values[:LIVE].astype(jnp.bfloat16)
        out_ref[to, 2 * LIVE :] = half


def regroup_kernel(blocks_ref, out_ref):
    for to in range(X):
        for z in range(Z):
            out_ref[to, z * LIVE : (z + 1) * LIVE] = blocks_ref[z, :LIVE]
            out_ref[to, LIST + z * LIVE : LIST + (z + 1) * LIVE] = blocks_ref[z, LIVE : 2 * LIVE]
        out_ref[to, 2 * LIST :] = blocks_ref[0, 2 * LIVE :]


def score(key_rows, stacked, at):
    return lax.dot_general(
        key_rows, stacked[at, :], (((1,), (1,)), ((), ())), preferred_element_type=jnp.float32
    )


def begin(keys_ref, values_ref, stacked, most_ref, total_ref):
    key = lax.broadcasted_iota(jnp.int32, (TOK, TILE), 0)
    causal = lax.broadcasted_iota(jnp.int32, (TOK, TILE), 1) % TOK >= key
    turned = jnp.transpose(values_ref[...].astype(jnp.float32))
    value_rows = jnp.concatenate([turned, jnp.ones((ONES, TOK), jnp.float32)]).astype(jnp.bfloat16)
    for tile in range(ROWS // TILE):
        at = slice(tile * TILE, (tile + 1) * TILE)
        scores = jnp.where(causal, score(keys_ref[...], stacked, at), NEG)
        most = jnp.max(scores, axis=0, keepdims=True)
        most_ref[:, at] = jnp.broadcast_to(most, (8, TILE))
        weights = jnp.exp2((scores - most) * SCALE).astype(jnp.bfloat16)
        total_ref[:, at] = jnp.dot(value_rows, weights, preferred_element_type=jnp.float32)


def fold(key_rows, value_rows, stacked, most_ref, total_ref, online):
    for tile in range(ROWS // TILE):
        at = slice(tile * TILE, (tile + 1) * TILE)
        scores = score(key_rows, stacked, at)
        most = most_ref[:1, at]
        if online:
            before = most
            most = jnp.maximum(before, jnp.max(scores, axis=0, keepdims=True))
            most_ref[:, at] = jnp.broadcast_to(most, (8, TILE))
            total_ref[:, at] = total_ref[:, at] * jnp.exp2((before - most) * SCALE)
        weights = jnp.exp2((scores - most) * SCALE).astype(jnp.bfloat16)
        total_ref[:, at] += jnp.dot(value_rows, weights, preferred_element_type=jnp.float32)


def sound(total_ref):
    return jnp.max(jnp.where(total_ref[HD : HD + 8, :] < SAFE, 0.0, 1.0)) < 0.5


def fill(stacked, queries_ref):
    for head in range(GROUP):
        stacked[head * TOK : (head + 1) * TOK, :] = queries_ref[:, head * HD : (head + 1) * HD]


def marked(values, live):
    turned = jnp.transpose(values)
    ok = (turned < LIMIT) & (lax.broadcasted_iota(jnp.int32, turned.shape, 1) < live)
    kept = jnp.where(ok, turned, 0.0)
    return jnp.concatenate([kept, jnp.where(ok[:ONES], 1.0, 0.0)]).astype(jnp.bfloat16)


def columns(core, stand_in, columns_ref, stacked, most_ref, total_ref, online):
    own_z = lax.axis_index("z")
    own_side = lax.axis_index("x") * C + lax.axis_index("core")
    row = lax.broadcasted_iota(jnp.int32, (LIST, HD), 0)

    def column(x, carry):
        live = (own_z + (x * C + core < own_side).astype(jnp.int32)) * LIVE
        key_rows = columns_ref[x, :LIST].astype(jnp.float32)
        key_rows = jnp.where(row < live, key_rows, stand_in).astype(jnp.bfloat16)
        value_rows = marked(columns_ref[x, LIST : 2 * LIST].astype(jnp.float32), live)
        fold(key_rows, value_rows, stacked, most_ref, total_ref, online)
        return carry

    lax.fori_loop(0, X, column, 0, unroll=not online)


def near_kernel(queries_ref, keys_ref, values_ref, columns_ref, most_ref, total_ref, stacked):
    fill(stacked, queries_ref)
    stand_in = keys_ref[:1].astype(jnp.float32)

    def go(online):
        begin(keys_ref, values_ref, stacked, most_ref, total_ref)
        core = lax.axis_index("core")
        columns(core, stand_in, columns_ref, stacked, most_ref, total_ref, online)

    go(False)

    @pl.when(jnp.logical_not(sound(total_ref)))
    def _():
        go(True)


def far_kernel(queries_ref, keys_ref, mine_ref, columns_ref, most_in, total_in, out_ref, stacked, most_ref, total_ref):
    fill(stacked, queries_ref)
    stand_in = keys_ref[:1].astype(jnp.float32)
    even = lax.axis_index("core") == 0
    own = lax.axis_index("z") * (X * C) + lax.axis_index("x") * C + lax.axis_index("core")
    live = jnp.where(own > 0, ANCHOR, 0)

    def go(online):
        most_ref[...] = most_in[...]
        total_ref[...] = total_in[...]
        columns(1 - lax.axis_index("core"), stand_in, columns_ref, stacked, most_ref, total_ref, online)
        mine = mine_ref[...].astype(jnp.float32)
        other = columns_ref[0, 2 * LIST :].astype(jnp.float32)
        keep = lax.broadcasted_iota(jnp.int32, (ANCHOR, HD), 0) < live
        key_rows = jnp.where(keep, jnp.where(even, mine, other), stand_in).astype(jnp.bfloat16)
        value_rows = marked(jnp.where(even, other, mine), live)
        fold(key_rows, value_rows, stacked, most_ref, total_ref, online)

    go(False)

    @pl.when(jnp.logical_not(sound(total_ref)))
    def _():
        go(True)

    for head in range(GROUP):
        at = slice(head * TOK, (head + 1) * TOK)
        done = total_ref[:HD, at] / total_ref[HD : HD + 1, at]
        out_ref[:, head * HD : (head + 1) * HD] = jnp.transpose(done).astype(jnp.bfloat16)


def body(queries, keys, values, keep_index, keep_count):
    half = jnp.bfloat16
    passed = lax.ppermute(values, ("z", "x", "core"), [(0, 1)])
    blocks = call(
        pack_kernel,
        jax.ShapeDtypeStruct((Z, SLOT, HD), half),
        [HBM] * 4 + [VM],
        VM,
        [
            pltpu.SMEM((1, 1, 1), jnp.int32),
            pltpu.VMEM((1, 1, HD), jnp.int32),
            pltpu.VMEM((TOK, HD), half),
            pltpu.VMEM((TOK, HD), half),
            pltpu.SemaphoreType.DMA((4,)),
        ],
        1 << 24,
        60 << 20,
    )(keep_count, keep_index, keys, values, passed)
    blocks = lax.all_to_all(blocks.reshape(Z, SLOT // PIECE, PIECE, HD), "z", 0, 0, tiled=True)
    blocks = blocks.reshape(Z, SLOT, HD)
    column = call(regroup_kernel, jax.ShapeDtypeStruct((X, COLUMN, HD), half), [VM], VM)(blocks)
    column = column.reshape(X, COLUMN // PIECE, PIECE, HD)
    column = lax.all_to_all(column, "x", 0, 0, tiled=True).reshape(X, COLUMN, HD)
    other = lax.ppermute(column, "core", [(0, 1), (1, 0)])
    flops = 4 * ROWS * X * LIST * HD
    state = [pltpu.VMEM((8, ROWS), jnp.float32), pltpu.VMEM((HD + ONES, ROWS), jnp.float32)]
    most, total = call(
        near_kernel,
        tuple(jax.ShapeDtypeStruct((rows, ROWS), jnp.float32) for rows in (8, HD + ONES)),
        [VM] * 4,
        (VM, VM),
        [pltpu.VMEM((ROWS, HD), half)],
        flops,
    )(queries, keys, values, column)
    attended = call(
        far_kernel,
        jax.ShapeDtypeStruct((TOK, GROUP * HD), half),
        [VM] * 6,
        VM,
        [pltpu.VMEM((ROWS, HD), half)] + state,
        flops,
    )(queries, keys, column[0, 2 * LIST :], other, most, total)
    return lax.all_to_all(attended, "tensor", split_axis=0, concat_axis=1, tiled=True)


def solution(mesh):
    parts = Mesh(mesh.devices.reshape(Z, X, C, T), ("z", "x", "core", "tensor"))
    hosts = ("z", "x", "core")
    placed = (
        P(hosts, "tensor"),
        P(hosts, "tensor"),
        P(hosts, "tensor"),
        P(hosts, "tensor", None),
        P(hosts, "tensor", None),
    )
    return jax.shard_map(
        body, mesh=parts, in_specs=placed, out_specs=P(hosts + ("tensor",), None), check_vma=False
    )
```

time: 110 us -> 107 us (0.973)
  the two profiles are of different devices: /device:TPU:1 before, /device:TPU:3 now
where the time goes in v2:
time: 107 us; the launch traced here: 106 us
  blocking collectives  73.8 us (69%)
  Pallas kernels  24.4 us (23%)
  starting transfers between devices  5.86 us (5%)
  local copies, waits for them, and re-layouts  1.41 us (1%)
    all_to_all x1, blocking collectives, body(): lax.all_to_all(blocks.reshape(Z, SLOT // PIECE, PIECE, HD), 'z', 0, 0, ti...  29.2 us
    all_to_all x1, blocking collectives, body(): lax.all_to_all(column, 'x', 0, 0, tiled=True).reshape(X, COLUMN, HD)  22.8 us
    all_to_all x1, blocking collectives, body(): lax.all_to_all(attended, 'tensor', split_axis=0, concat_axis=1, tiled=True)  21.8 us
    pallas_call x1, Pallas kernels, body(): call(far_kernel, jax.ShapeDtypeStruct((TOK, GROUP * HD), half), [VM] * 6,...  15.9 us
    pallas_call x1, Pallas kernels, body(): call(near_kernel, tuple((jax.ShapeDtypeStruct((rows, ROWS), jnp.float32)...  5.39 us
    ppermute x1, starting transfers between devices, body(): other = lax.ppermute(column, 'core', [(0, 1), (1, 0)])  5.2 us
    pallas_call x1, Pallas kernels, body(): call(pack_kernel, jax.ShapeDtypeStruct((Z, SLOT, HD), half), [HBM] * 4 +...  2.84 us
  transfers between devices with their start and end apart: 2, of which 0 were waited for; matrix products, arithmetic and copies ran while one was open for 0% of the time, Pallas kernels for 5%

profile of v2, /device:TPU:3, one launch (start us, length us, event | category | flops | bytes accessed | tf_op | source)
XLA Modules:
  0.0 106.2 jit_solution(4653776340466977346)
XLA Ops:
  0.0 0.7 collective-permute-start
  1.3 0.0 collective-permute-done.passed_ref
  1.3 0.0 copy-start.3
  1.3 0.6 copy-done.3
  1.9 2.8 %shard_map.55 = bf16[8,320,128]{2,1,0:T(8,128)(2,1)} custom-call(s32[1,1,1]{2,1,0:T(1,128)S(6)} %copy.8.count_in, s32[1,1,128]{2,1,0:T(1,128)} %index_in.1, bf16[192,128]{1,0:T(8,128)(2,1)} %keys_ref.3, bf16[192,128]{1,0:T(8,128)(2,1)} %values_ref.1, bf16[192,128]{1,0:T(8,128)(2,1)} %copy-done.3), custom_call_target="tpu_custom_call" | custom-call | flops 16777216 | bytes 1048576 | tf_op jit(solution)/shard_map/pallas_call | solution.py:208
  4.8 29.2 %all_to_all.29 = bf16[8,20,16,128]{3,2,1,0:T(8,128)(2,1)S(1)} all-to-all(bf16[8,20,16,128]{3,2,1,0:T(8,128)(2,1)} %bitcast.16), channel_id=1, replica_groups=mesh['z'=8,'x'=4,'core'=2,'tensor'=8] {'z'}, dimensions={0} | all-to-all | bytes 1310720 | tf_op jit(solution)/shard_map/all_to_all | solution.py:223
  34.0 0.2 shard_map.56
  34.2 0.0 copy-start
  34.2 0.0 copy-start.1
  34.2 0.0 copy-start.2
  34.2 22.8 %all_to_all.30 = bf16[4,104,16,128]{3,2,1,0:T(8,128)(2,1)S(1)} all-to-all(bf16[4,104,16,128]{3,2,1,0:T(8,128)(2,1)S(1)} %bitcast.10), channel_id=1, replica_groups=mesh['z'=8,'x'=4,'core'=2,'tensor'=8] {'x'}, dimensions={0} | all-to-all | bytes 3407872 | tf_op jit(solution)/shard_map/all_to_all | solution.py:227
  57.0 5.2 %collective-permute-start.1 = (bf16[4,1664,128]{2,1,0:T(8,128)(2,1)S(1)}, bf16[4,1664,128]{2,1,0:T(8,128)(2,1)S(1)}, u32[]{:S(2)}, u32[]{:S(2)}) collective-permute-start(bf16[4,1664,128]{2,1,0:T(8,128)(2,1)S(1)} %bitcast.12), channel_id=1, source_target_pairs={{0,8},{8,0},{1,9},{9,1},{2,10},{10,2},{3,11},{11,3},{4,12},{12,4},... | collective-permute-start | bytes 5111816 | tf_op jit(solution)/shard_map/ppermute | solution.py:228
  62.3 0.0 copy-done
  62.3 0.0 copy-done.1
  62.3 0.0 copy-done.2
  62.3 5.4 %shard_map.57 = (f32[8,1536]{1,0:T(8,128)S(1)}, f32[136,1536]{1,0:T(8,128)S(1)}) custom-call(bf16[192,1024]{1,0:T(8,128)(2,1)S(1)} %copy-done.2, bf16[192,128]{1,0:T(8,128)(2,1)S(1)} %copy-done.1, bf16[192,128]{1,0:T(8,128)(2,1)S(1)} %copy-done, bf16[4,1664,128]{2,1,0:T(8,128)(2,1)S(1)} %bitcast.14), custom_call_target="tpu_custom_call" | custom-call | flops 2415919104 | bytes 1048576 | tf_op jit(solution)/shard_map/pallas_call | solution.py:231
  67.7 0.0 collective-permute-done.1.columns_ref
  67.7 15.9 %shard_map.58 = bf16[192,1024]{1,0:T(8,128)(2,1)S(1)} custom-call(bf16[192,1024]{1,0:T(8,128)(2,1)S(1)} %copy-done.2, bf16[192,128]{1,0:T(8,128)(2,1)S(1)} %copy-done.1, bf16[128,128]{1,0:T(8,128)(2,1)S(1)} %slice_bitcast_fusion.mine_ref, bf16[4,1664,128]{2,1,0:T(8,128)(2,1)S(1)} %collective-permute-done.1.columns_ref, ...), custom_call_target="tpu_custom_call" | custom-call | flops 2415919104 | bytes 1048576 | tf_op jit(solution)/shard_map/pallas_call | solution.py:239
  83.6 21.8 %all_to_all.31 = bf16[8,24,1024]{2,1,0:T(8,128)(2,1)S(1)} all-to-all(bf16[8,24,1024]{2,1,0:T(8,128)(2,1)S(1)} %bitcast.15), channel_id=1, replica_groups=mesh['z'=8,'x'=4,'core'=2,'tensor'=8] {'tensor'}, dimensions={0} | all-to-all | bytes 786432 | tf_op jit(solution)/shard_map/all_to_all | solution.py:247
  105.4 0.8 copy.7
  (1 shorter events, 0.0 us)
Async XLA Ops:
  0.0 1.3 %collective-permute-start = (bf16[192,128]{1,0:T(8,128)(2,1)}, bf16[192,128]{1,0:T(8,128)(2,1)S(1)}, u32[]{:S(2)}, u32[]{:S(2)}) collective-permute-start(bf16[192,128]{1,0:T(8,128)(2,1)} %values_ref.1), channel_id=1, source_target_pairs={{0,8},{1,9},{2,10},{3,11},{4,12},{5,13},{6,14},{7,15}} | collective-permute-start | bytes 147464 | tf_op jit(solution)/shard_map/ppermute | solution.py:207
  1.3 0.6 copy-start.3
  34.2 28.0 %copy-start = (bf16[192,128]{1,0:T(8,128)(2,1)S(1)}, bf16[192,128]{1,0:T(8,128)(2,1)}, u32[]{:S(2)}) copy-start(bf16[192,128]{1,0:T(8,128)(2,1)} %values_ref.1) | copy-start | bytes 147460
  34.2 28.0 %copy-start.1 = (bf16[192,128]{1,0:T(8,128)(2,1)S(1)}, bf16[192,128]{1,0:T(8,128)(2,1)}, u32[]{:S(2)}) copy-start(bf16[192,128]{1,0:T(8,128)(2,1)} %keys_ref.3) | copy-start | bytes 147460
  34.2 28.0 %copy-start.2 = (bf16[192,1024]{1,0:T(8,128)(2,1)S(1)}, bf16[192,1024]{1,0:T(8,128)(2,1)}, u32[]{:S(2)}) copy-start(bf16[192,1024]{1,0:T(8,128)(2,1)} %queries_ref.3) | copy-start | bytes 1179652
  57.0 10.7 %collective-permute-start.1 = (bf16[4,1664,128]{2,1,0:T(8,128)(2,1)S(1)}, bf16[4,1664,128]{2,1,0:T(8,128)(2,1)S(1)}, u32[]{:S(2)}, u32[]{:S(2)}) collective-permute-start(bf16[4,1664,128]{2,1,0:T(8,128)(2,1)S(1)} %bitcast.12), channel_id=1, source_target_pairs={{0,8},{8,0},{1,9},{9,1},{2,10},{10,2},{3,11},{11,3},{4,12},{12,4},... | collective-permute-start | bytes 5111816 | tf_op jit(solution)/shard_map/ppermute | solution.py:228

commit v3 on v2

v3 whole, which is shorter than its diff:
```python
import jax
import jax.numpy as jnp
from jax import lax
from jax.experimental import pallas as pl
from jax.experimental.pallas import tpu as pltpu
from jax.sharding import Mesh, PartitionSpec as P

QH = 64
KVH = 8
HD = 128
TOK = 192
ANCHOR = 128
GROUP = QH // KVH
ROWS = GROUP * TOK
LIVE = 96
MARK = 16.0
LIMIT = 8.0
Z, X, C, T = 8, 4, 2, 8
SLOT = 2 * LIVE
LIST = Z * LIVE
COLUMN = 2 * LIST
LEAD = (Z * X - 1) * C
PIECE = 16
TILE = 768
ONES = 8
SAFE = 2.0**100
NEG = -1e30
LOG2E = 1.4426950408889634
SCALE = HD ** (-0.5) * LOG2E
LIMIT_BYTES = 40 * 1024 * 1024

VM = pl.BlockSpec(memory_space=pltpu.VMEM)


def call(kernel, out_shape, in_specs, out_specs, scratch=(), flops=0):
    return pl.pallas_call(
        kernel,
        out_shape=out_shape,
        in_specs=in_specs,
        out_specs=out_specs,
        scratch_shapes=list(scratch),
        compiler_params=pltpu.CompilerParams(vmem_limit_bytes=LIMIT_BYTES),
        cost_estimate=pl.CostEstimate(flops=flops, bytes_accessed=1 << 20, transcendentals=0),
    )


def lead_half(passed_keys_ref, passed_values_ref):
    even = lax.axis_index("core") == 0
    half = jnp.where(
        even,
        passed_keys_ref[:ANCHOR].astype(jnp.float32),
        passed_values_ref[:ANCHOR].astype(jnp.float32),
    )
    return half.astype(jnp.bfloat16)


def pack_kernel(picks_ref, pair_ref, passed_keys_ref, passed_values_ref, out_ref):
    slots, count = picks_ref[0, :, :HD], picks_ref[0, :, HD : HD + 1]
    lane = lax.broadcasted_iota(jnp.int32, (1, HD), 1)
    picks = jnp.where(lane < count, slots, slots[:, :1])
    row = lax.broadcasted_iota(jnp.int32, (TOK, HD), 0)
    contract = (((0,), (0,)), ((), ()))
    hot = (row == picks).astype(jnp.float32).astype(jnp.bfloat16)
    picked = lax.dot_general(hot, pair_ref[...], contract, preferred_element_type=jnp.float32)
    slot = lax.broadcasted_iota(jnp.int32, (HD, HD), 0)
    picked_keys = picked[:LIVE, :HD].astype(jnp.bfloat16)
    picked_values = jnp.where(slot < count, picked[:, HD:], MARK)[:LIVE].astype(jnp.bfloat16)
    for to in range(Z):
        out_ref[to, :LIVE] = picked_keys
        out_ref[to, LIVE:] = picked_values

    @pl.when((lax.axis_index("z") == Z - 1) & (lax.axis_index("x") == X - 1))
    def _():
        half = lead_half(passed_keys_ref, passed_values_ref)
        for to in range(Z - 1):
            out_ref[to, :ANCHOR] = half


def regroup_kernel(blocks_ref, passed_keys_ref, passed_values_ref, out_ref):
    for to in range(X):
        for z in range(Z):
            out_ref[to, z * LIVE : (z + 1) * LIVE] = blocks_ref[z, :LIVE]
            out_ref[to, LIST + z * LIVE : LIST + (z + 1) * LIVE] = blocks_ref[z, LIVE:]
    z, last = lax.axis_index("z"), lax.axis_index("x") == X - 1

    def put(to, half):
        at = pl.multiple_of(z * LIVE, 32)
        out_ref[to, pl.ds(at, LIVE)] = half[:LIVE]
        out_ref[to, pl.ds(pl.multiple_of(LIST + at, 32), ANCHOR - LIVE)] = half[LIVE:]

    @pl.when(last & (z < Z - 1))
    def _():
        for to in range(X - 1):
            put(to, blocks_ref[Z - 1, :ANCHOR])

    @pl.when(last & (z == Z - 1))
    def _():
        half = lead_half(passed_keys_ref, passed_values_ref)
        for to in range(X - 1):
            put(to, half)

        @pl.when(lax.axis_index("core") == C - 1)
        def _():
            put(X - 1, half)


def anchor_half(columns_ref):
    place = jnp.where(lax.axis_index("x") == X - 1, Z - 1, lax.axis_index("z"))
    at = pl.multiple_of(place * LIVE, 32)
    low = columns_ref[X - 1, pl.ds(at, LIVE)].astype(jnp.float32)
    high = columns_ref[X - 1, pl.ds(pl.multiple_of(LIST + at, 32), ANCHOR - LIVE)]
    return jnp.concatenate([low, high.astype(jnp.float32)])


def score(key_rows, stacked, at):
    return lax.dot_general(
        key_rows, stacked[at, :], (((1,), (1,)), ((), ())), preferred_element_type=jnp.float32
    )


def begin(keys_ref, values_ref, stacked, most_ref, total_ref):
    key = lax.broadcasted_iota(jnp.int32, (TOK, TILE), 0)
    causal = lax.broadcasted_iota(jnp.int32, (1, TILE), 1) % TOK >= key
    turned = jnp.transpose(values_ref[...].astype(jnp.float32))
    value_rows = jnp.concatenate([turned, jnp.ones((ONES, TOK), jnp.float32)]).astype(jnp.bfloat16)
    for tile in range(ROWS // TILE):
        at = slice(tile * TILE, (tile + 1) * TILE)
        scores = jnp.where(causal, score(keys_ref[...], stacked, at), NEG)
        most = jnp.max(scores, axis=0, keepdims=True)
        most_ref[:, at] = jnp.broadcast_to(most, (8, TILE))
        weights = jnp.exp2((scores - most) * SCALE).astype(jnp.bfloat16)
        total_ref[:, at] = jnp.dot(value_rows, weights, preferred_element_type=jnp.float32)


def fold(key_rows, value_rows, stacked, most_ref, total_ref, source, online):
    for tile in range(ROWS // TILE):
        at = slice(tile * TILE, (tile + 1) * TILE)
        scores = score(key_rows, stacked, at)
        most = most_ref[:1, at]
        total = source[:, at]
        if online:
            before = most
            most = jnp.maximum(before, jnp.max(scores, axis=0, keepdims=True))
            most_ref[:, at] = jnp.broadcast_to(most, (8, TILE))
            total = total * jnp.exp2((before - most) * SCALE)
        weights = jnp.exp2((scores - most) * SCALE).astype(jnp.bfloat16)
        total_ref[:, at] = total + jnp.dot(value_rows, weights, preferred_element_type=jnp.float32)


def sound(total_ref):
    return jnp.max(jnp.where(total_ref[HD : HD + 8, :] < SAFE, 0.0, 1.0)) < 0.5


def fill(stacked, queries_ref):
    for head in range(GROUP):
        stacked[head * TOK : (head + 1) * TOK, :] = queries_ref[:, head * HD : (head + 1) * HD]


def marked(values, live):
    turned = jnp.transpose(values)
    ok = (turned < LIMIT) & (lax.broadcasted_iota(jnp.int32, turned.shape, 1) < live)
    kept = jnp.where(ok, turned, 0.0)
    return jnp.concatenate([kept, jnp.where(ok[:ONES], 1.0, 0.0)]).astype(jnp.bfloat16)


def columns(core, stand_in, columns_ref, stacked, most_ref, total_ref, online):
    own_z = lax.axis_index("z")
    own_side = lax.axis_index("x") * C + lax.axis_index("core")
    row = lax.broadcasted_iota(jnp.int32, (LIST, HD), 0)

    def column(x, carry):
        live = (own_z + (x * C + core < own_side).astype(jnp.int32)) * LIVE
        key_rows = columns_ref[x, :LIST].astype(jnp.float32)
        key_rows = jnp.where(row < live, key_rows, stand_in).astype(jnp.bfloat16)
        value_rows = marked(columns_ref[x, LIST : 2 * LIST].astype(jnp.float32), live)
        fold(key_rows, value_rows, stacked, most_ref, total_ref, total_ref, online)
        return carry

    lax.fori_loop(0, X, column, 0, unroll=not online)


def near_kernel(queries_ref, keys_ref, values_ref, columns_ref, most_ref, total_ref, stacked):
    fill(stacked, queries_ref)
    stand_in = keys_ref[:1].astype(jnp.float32)

    def go(online):
        begin(keys_ref, values_ref, stacked, most_ref, total_ref)
        core = lax.axis_index("core")
        columns(core, stand_in, columns_ref, stacked, most_ref, total_ref, online)

    go(False)

    @pl.when(jnp.logical_not(sound(total_ref)))
    def _():
        go(True)


def far_kernel(
    stacked,
    keys_ref,
    passed_keys_ref,
    passed_values_ref,
    extra_keys_ref,
    near_ref,
    columns_ref,
    most_in,
    total_in,
    out_ref,
    most_ref,
    total_ref,
):
    stand_in = keys_ref[:1].astype(jnp.float32)
    even = lax.axis_index("core") == 0
    own = lax.axis_index("z") * (X * C) + lax.axis_index("x") * C + lax.axis_index("core")
    live = jnp.where(own > 0, ANCHOR, 0)

    def go(online):
        most_ref[...] = most_in[...]
        mine, other = anchor_half(near_ref), anchor_half(columns_ref)
        lead_keys = jnp.where(
            even,
            passed_keys_ref[:ANCHOR].astype(jnp.float32),
            extra_keys_ref[:ANCHOR].astype(jnp.float32),
        )
        anchor_keys = jnp.where(own >= LEAD, lead_keys, jnp.where(even, mine, other))
        anchor_values = jnp.where(even, other, mine)
        anchor_values = jnp.where(
            own == LEAD + 1, passed_values_ref[:ANCHOR].astype(jnp.float32), anchor_values
        )
        keep = lax.broadcasted_iota(jnp.int32, (ANCHOR, HD), 0) < live
        key_rows = jnp.where(keep, anchor_keys, stand_in).astype(jnp.bfloat16)
        value_rows = marked(anchor_values, live)
        fold(key_rows, value_rows, stacked, most_ref, total_ref, total_in, online)
        columns(1 - lax.axis_index("core"), stand_in, columns_ref, stacked, most_ref, total_ref, online)

    go(False)

    @pl.when(jnp.logical_not(sound(total_ref)))
    def _():
        go(True)

    for head in range(GROUP):
        at = slice(head * TOK, (head + 1) * TOK)
        done = total_ref[:HD, at] * (1.0 / total_ref[HD : HD + 1, at])
        out_ref[:, head * HD : (head + 1) * HD] = jnp.transpose(done).astype(jnp.bfloat16)


def body(queries, keys, values, keep_index, keep_count):
    half = jnp.bfloat16
    hosts = ("z", "x", "core")
    passed_keys = lax.ppermute(keys, hosts, [(0, LEAD)])
    passed_values = lax.ppermute(values, hosts, [(0, LEAD + 1)])
    extra_keys = lax.ppermute(keys, hosts, [(0, LEAD + 1)])
    picks = jnp.concatenate([keep_index, keep_count], axis=2)
    pair = jnp.concatenate([keys, values], axis=1)
    blocks = call(
        pack_kernel, jax.ShapeDtypeStruct((Z, SLOT, HD), half), [VM] * 4, VM, flops=1 << 24
    )(picks, pair, passed_keys, passed_values)
    blocks = lax.all_to_all(blocks.reshape(Z, SLOT // PIECE, PIECE, HD), "z", 0, 0, tiled=True)
    blocks = blocks.reshape(Z, SLOT, HD)
    column = call(regroup_kernel, jax.ShapeDtypeStruct((X, COLUMN, HD), half), [VM] * 3, VM)(
        blocks, passed_keys, passed_values
    )
    column = column.reshape(X, COLUMN // PIECE, PIECE, HD)
    column = lax.all_to_all(column, "x", 0, 0, tiled=True).reshape(X, COLUMN, HD)
    other = lax.ppermute(column, "core", [(0, 1), (1, 0)])
    flops = 4 * ROWS * X * LIST * HD
    state = [pltpu.VMEM((8, ROWS), jnp.float32), pltpu.VMEM((HD + ONES, ROWS), jnp.float32)]
    most, total, stacked = call(
        near_kernel,
        tuple(jax.ShapeDtypeStruct((rows, ROWS), jnp.float32) for rows in (8, HD + ONES))
        + (jax.ShapeDtypeStruct((ROWS, HD), half),),
        [VM] * 4,
        (VM,) * 3,
        flops=flops,
    )(queries, keys, values, column)
    attended = call(
        far_kernel,
        jax.ShapeDtypeStruct((TOK, GROUP * HD), half),
        [VM] * 9,
        VM,
        state,
        flops,
    )(stacked, keys, passed_keys, passed_values, extra_keys, column, other, most, total)
    return lax.all_to_all(attended, "tensor", split_axis=0, concat_axis=1, tiled=True)


def solution(mesh):
    parts = Mesh(mesh.devices.reshape(Z, X, C, T), ("z", "x", "core", "tensor"))
    hosts = ("z", "x", "core")
    placed = (
        P(hosts, "tensor"),
        P(hosts, "tensor"),
        P(hosts, "tensor"),
        P(hosts, "tensor", None),
        P(hosts, "tensor", None),
    )
    return jax.shard_map(
        body, mesh=parts, in_specs=placed, out_specs=P(hosts + ("tensor",), None), check_vma=False
    )
```

time: 107 us -> 102 us (0.953)
  blocking collectives: 73.8 us -> 66.3 us
  starting transfers between devices: 5.86 us -> 10.1 us
  Pallas kernels: 24.4 us -> 21.8 us
  other arithmetic: 0 us -> 1.5 us
    all_to_all x1, blocking collectives: 29.2 us -> 23.3 us  [body(): lax.all_to_all(blocks.reshape(Z, SLOT // PIECE, PIECE, HD), 'z', 0, 0, ti...]
    ppermute x1, starting transfers between devices: 5.2 us -> 8.16 us  [body(): other = lax.ppermute(column, 'core', [(0, 1), (1, 0)])]
    pallas_call x3, Pallas kernels: 19 us -> 16.4 us  [the longest x1 15.9 us: body(): call(far_kernel, jax.ShapeDtypeStruct((TOK, GROUP * HD), half), [VM] * 9,...]
    all_to_all x1, blocking collectives: 22.8 us -> 21.2 us  [body(): lax.all_to_all(column, 'x', 0, 0, tiled=True).reshape(X, COLUMN, HD)]
    concatenate x0 -> x2, other arithmetic: none -> 1.5 us  [the longest x1 0.84 us: body(): pair = jnp.concatenate([keys, values], axis=1)]
    ppermute x1 -> x3, starting transfers between devices: 0.65 us -> 1.98 us  [the longest x1 0.66 us: body(): passed_keys = lax.ppermute(keys, hosts, [(0, LEAD)])]
  transfers between devices with their start and end apart: 2 -> 4, of which waited for: 0 -> 0; matrix products, arithmetic and copies ran while one was open for 0% -> 1% of each run, Pallas kernels for 5% -> 5%
where the time goes in v3:
time: 102 us; the launch traced here: 101 us
  blocking collectives  66.3 us (65%)
  Pallas kernels  21.8 us (21%)
  starting transfers between devices  10.1 us (10%)
  other arithmetic  1.5 us (1%)
    all_to_all x1, blocking collectives, body(): lax.all_to_all(blocks.reshape(Z, SLOT // PIECE, PIECE, HD), 'z', 0, 0, ti...  23.3 us
    all_to_all x1, blocking collectives, body(): lax.all_to_all(attended, 'tensor', split_axis=0, concat_axis=1, tiled=True)  21.8 us
    all_to_all x1, blocking collectives, body(): lax.all_to_all(column, 'x', 0, 0, tiled=True).reshape(X, COLUMN, HD)  21.2 us
    pallas_call x1, Pallas kernels, body(): call(far_kernel, jax.ShapeDtypeStruct((TOK, GROUP * HD), half), [VM] * 9,...  15.9 us
    ppermute x1, starting transfers between devices, body(): other = lax.ppermute(column, 'core', [(0, 1), (1, 0)])  8.16 us
    pallas_call x1, Pallas kernels, body(): call(near_kernel, tuple((jax.ShapeDtypeStruct((rows, ROWS), jnp.float32)...  5.41 us
  transfers between devices with their start and end apart: 4, of which 0 were waited for; matrix products, arithmetic and copies ran while one was open for 1% of the time, Pallas kernels for 5%

profile of v3, /device:TPU:3, one launch (start us, length us, event | category | flops | bytes accessed | tf_op | source)
XLA Modules:
  0.0 101.4 jit_solution(749620603136106281)
XLA Ops:
  0.0 0.7 collective-permute-start.1
  0.7 0.7 collective-permute-start
  1.3 0.8 pad_maximum_fusion.pair_ref
  2.8 0.7 pad_add_fusion.picks_ref
  3.5 0.0 collective-permute-done.1.passed_values_ref
  3.5 0.0 collective-permute-done.passed_keys_ref
  3.5 0.3 shard_map.55
  3.8 23.3 %all_to_all.29 = bf16[8,12,16,128]{3,2,1,0:T(8,128)(2,1)S(1)} all-to-all(bf16[8,12,16,128]{3,2,1,0:T(8,128)(2,1)S(1)} %bitcast.12), channel_id=1, replica_groups=mesh['z'=8,'x'=4,'core'=2,'tensor'=8] {'z'}, dimensions={0} | all-to-all | bytes 786432 | tf_op jit(solution)/shard_map/all_to_all | solution.py:259
  27.1 0.2 shard_map.56
  27.3 0.0 copy-start.1
  27.4 0.0 copy-start
  27.4 0.0 copy-start.2
  27.4 21.2 %all_to_all.30 = bf16[4,96,16,128]{3,2,1,0:T(8,128)(2,1)S(1)} all-to-all(bf16[4,96,16,128]{3,2,1,0:T(8,128)(2,1)S(1)} %bitcast.8), channel_id=1, replica_groups=mesh['z'=8,'x'=4,'core'=2,'tensor'=8] {'x'}, dimensions={0} | all-to-all | bytes 3145728 | tf_op jit(solution)/shard_map/all_to_all | solution.py:265
  48.6 8.2 %collective-permute-start.3 = (bf16[4,1536,128]{2,1,0:T(8,128)(2,1)S(1)}, bf16[4,1536,128]{2,1,0:T(8,128)(2,1)S(1)}, u32[]{:S(2)}, u32[]{:S(2)}) collective-permute-start(bf16[4,1536,128]{2,1,0:T(8,128)(2,1)S(1)} %bitcast.9), channel_id=1, source_target_pairs={{0,8},{8,0},{1,9},{9,1},{2,10},{10,2},{3,11},{11,3},{4,12},{12,4},... | collective-permute-start | bytes 4718600 | tf_op jit(solution)/shard_map/ppermute | solution.py:266
  56.7 0.0 copy-done.1
  56.7 0.7 collective-permute-start.2
  57.4 0.0 copy-done
  57.4 0.0 copy-done.2
  57.4 5.4 %shard_map.57 = (f32[8,1536]{1,0:T(8,128)S(1)}, f32[136,1536]{1,0:T(8,128)S(1)}, bf16[1536,128]{1,0:T(8,128)(2,1)S(1)}) custom-call(bf16[192,1024]{1,0:T(8,128)(2,1)S(1)} %copy-done.2, bf16[192,128]{1,0:T(8,128)(2,1)S(1)} %copy-done.1, bf16[192,128]{1,0:T(8,128)(2,1)S(1)} %copy-done, bf16[4,1536,128]{2,1,0:T(8,128)(2,1)S(1)} %bitcast.10), custom_call_target="tpu_custom_call" | custom-call | flops 2415919104 | bytes 1048576 | tf_op jit(solution)/shard_map/pallas_call | solution.py:269
  62.8 0.0 collective-permute-done.2.extra_keys_ref
  62.8 0.0 collective-permute-done.3.columns_ref
  62.9 15.9 %shard_map.58 = bf16[192,1024]{1,0:T(8,128)(2,1)S(1)} custom-call(bf16[1536,128]{1,0:T(8,128)(2,1)S(1)} %get-tuple-element.8.stacked, bf16[192,128]{1,0:T(8,128)(2,1)S(1)} %copy-done.1, bf16[192,128]{1,0:T(8,128)(2,1)S(1)} %collective-permute-done.passed_keys_ref, bf16[192,128]{1,0:T(8,128)(2,1)S(1)} %collective-permute-done.1.passed_values_ref, ...), custom_call_target="tpu_custom_call" | custom-call | flops 2415919104 | bytes 1048576 | tf_op jit(solution)/shard_map/pallas_call | solution.py:277
  78.8 21.8 %all_to_all.31 = bf16[8,24,1024]{2,1,0:T(8,128)(2,1)S(1)} all-to-all(bf16[8,24,1024]{2,1,0:T(8,128)(2,1)S(1)} %bitcast.14), channel_id=1, replica_groups=mesh['z'=8,'x'=4,'core'=2,'tensor'=8] {'tensor'}, dimensions={0} | all-to-all | bytes 786432 | tf_op jit(solution)/shard_map/all_to_all | solution.py:285
  100.6 0.8 copy.7
Async XLA Ops:
  0.0 3.5 %collective-permute-start.1 = (bf16[192,128]{1,0:T(8,128)(2,1)}, bf16[192,128]{1,0:T(8,128)(2,1)S(1)}, u32[]{:S(2)}, u32[]{:S(2)}) collective-permute-start(bf16[192,128]{1,0:T(8,128)(2,1)} %values_ref.1), channel_id=1, source_target_pairs={{0,504},{1,505},{2,506},{3,507},{4,508},{5,509},{6,510},{7,511}} | collective-permute-start | bytes 147464 | tf_op jit(solution)/shard_map/ppermute | solution.py:252
  0.7 2.8 %collective-permute-start = (bf16[192,128]{1,0:T(8,128)(2,1)}, bf16[192,128]{1,0:T(8,128)(2,1)S(1)}, u32[]{:S(2)}, u32[]{:S(2)}) collective-permute-start(bf16[192,128]{1,0:T(8,128)(2,1)} %keys_ref.3), channel_id=1, source_target_pairs={{0,496},{1,497},{2,498},{3,499},{4,500},{5,501},{6,502},{7,503}} | collective-permute-start | bytes 147464 | tf_op jit(solution)/shard_map/ppermute | solution.py:251
  27.3 29.4 %copy-start.1 = (bf16[192,128]{1,0:T(8,128)(2,1)S(1)}, bf16[192,128]{1,0:T(8,128)(2,1)}, u32[]{:S(2)}) copy-start(bf16[192,128]{1,0:T(8,128)(2,1)} %keys_ref.3) | copy-start | bytes 147460
  27.4 30.0 %copy-start = (bf16[192,128]{1,0:T(8,128)(2,1)S(1)}, bf16[192,128]{1,0:T(8,128)(2,1)}, u32[]{:S(2)}) copy-start(bf16[192,128]{1,0:T(8,128)(2,1)} %values_ref.1) | copy-start | bytes 147460
  27.4 30.0 %copy-start.2 = (bf16[192,1024]{1,0:T(8,128)(2,1)S(1)}, bf16[192,1024]{1,0:T(8,128)(2,1)}, u32[]{:S(2)}) copy-start(bf16[192,1024]{1,0:T(8,128)(2,1)} %queries_ref.1) | copy-start | bytes 1179652
  48.6 14.3 %collective-permute-start.3 = (bf16[4,1536,128]{2,1,0:T(8,128)(2,1)S(1)}, bf16[4,1536,128]{2,1,0:T(8,128)(2,1)S(1)}, u32[]{:S(2)}, u32[]{:S(2)}) collective-permute-start(bf16[4,1536,128]{2,1,0:T(8,128)(2,1)S(1)} %bitcast.9), channel_id=1, source_target_pairs={{0,8},{8,0},{1,9},{9,1},{2,10},{10,2},{3,11},{11,3},{4,12},{12,4},... | collective-permute-start | bytes 4718600 | tf_op jit(solution)/shard_map/ppermute | solution.py:266
  56.7 6.1 %collective-permute-start.2 = (bf16[192,128]{1,0:T(8,128)(2,1)S(1)}, bf16[192,128]{1,0:T(8,128)(2,1)S(1)}, u32[]{:S(2)}, u32[]{:S(2)}) collective-permute-start(bf16[192,128]{1,0:T(8,128)(2,1)S(1)} %copy-done.1), channel_id=1, source_target_pairs={{0,504},{1,505},{2,506},{3,507},{4,508},{5,509},{6,510},{7,511}} | collective-permute-start | bytes 147464 | tf_op jit(solution)/shard_map/ppermute | solution.py:253

commit v4 on v3

--- a/solution.py
+++ b/solution.py
@@ -107,8 +107,9 @@
 def anchor_half(columns_ref):
     place = jnp.where(lax.axis_index("x") == X - 1, Z - 1, lax.axis_index("z"))
     at = pl.multiple_of(place * LIVE, 32)
-    low = columns_ref[X - 1, pl.ds(at, LIVE)].astype(jnp.float32)
-    high = columns_ref[X - 1, pl.ds(pl.multiple_of(LIST + at, 32), ANCHOR - LIVE)]
+    at = pl.multiple_of((X - 1) * COLUMN + at, 32)
+    low = columns_ref[pl.ds(at, LIVE)].astype(jnp.float32)
+    high = columns_ref[pl.ds(pl.multiple_of(LIST + at, 32), ANCHOR - LIVE)]
     return jnp.concatenate([low, high.astype(jnp.float32)])
 
 
@@ -170,9 +171,11 @@
 
     def column(x, carry):
         live = (own_z + (x * C + core < own_side).astype(jnp.int32)) * LIVE
-        key_rows = columns_ref[x, :LIST].astype(jnp.float32)
+        at = pl.multiple_of(x * COLUMN, 32)
+        key_rows = columns_ref[pl.ds(at, LIST)].astype(jnp.float32)
         key_rows = jnp.where(row < live, key_rows, stand_in).astype(jnp.bfloat16)
-        value_rows = marked(columns_ref[x, LIST : 2 * LIST].astype(jnp.float32), live)
+        value_rows = columns_ref[pl.ds(pl.multiple_of(at + LIST, 32), LIST)].astype(jnp.float32)
+        value_rows = marked(value_rows, live)
         fold(key_rows, value_rows, stacked, most_ref, total_ref, total_ref, online)
         return carry
 
@@ -200,7 +203,6 @@
     keys_ref,
     passed_keys_ref,
     passed_values_ref,
-    extra_keys_ref,
     near_ref,
     columns_ref,
     most_in,
@@ -220,7 +222,7 @@
         lead_keys = jnp.where(
             even,
             passed_keys_ref[:ANCHOR].astype(jnp.float32),
-            extra_keys_ref[:ANCHOR].astype(jnp.float32),
+            columns_ref[X * COLUMN : X * COLUMN + ANCHOR].astype(jnp.float32),
         )
         anchor_keys = jnp.where(own >= LEAD, lead_keys, jnp.where(even, mine, other))
         anchor_values = jnp.where(even, other, mine)
@@ -250,7 +252,6 @@
     hosts = ("z", "x", "core")
     passed_keys = lax.ppermute(keys, hosts, [(0, LEAD)])
     passed_values = lax.ppermute(values, hosts, [(0, LEAD + 1)])
-    extra_keys = lax.ppermute(keys, hosts, [(0, LEAD + 1)])
     picks = jnp.concatenate([keep_index, keep_count], axis=2)
     pair = jnp.concatenate([keys, values], axis=1)
     blocks = call(
@@ -262,7 +263,8 @@
         blocks, passed_keys, passed_values
     )
     column = column.reshape(X, COLUMN // PIECE, PIECE, HD)
-    column = lax.all_to_all(column, "x", 0, 0, tiled=True).reshape(X, COLUMN, HD)
+    column = lax.all_to_all(column, "x", 0, 0, tiled=True)
+    column = jnp.concatenate([column.reshape(X * COLUMN, HD), passed_keys])
     other = lax.ppermute(column, "core", [(0, 1), (1, 0)])
     flops = 4 * ROWS * X * LIST * HD
     state = [pltpu.VMEM((8, ROWS), jnp.float32), pltpu.VMEM((HD + ONES, ROWS), jnp.float32)]
@@ -277,11 +279,11 @@
     attended = call(
         far_kernel,
         jax.ShapeDtypeStruct((TOK, GROUP * HD), half),
-        [VM] * 9,
+        [VM] * 8,
         VM,
         state,
         flops,
-    )(stacked, keys, passed_keys, passed_values, extra_keys, column, other, most, total)
+    )(stacked, keys, passed_keys, passed_values, column, other, most, total)
     return lax.all_to_all(attended, "tensor", split_axis=0, concat_axis=1, tiled=True)
 
 

time: 102 us -> 101 us (level)
  transfers between devices with their start and end apart: 4 -> 3, of which waited for: 0 -> 0; matrix products, arithmetic and copies ran while one was open for 1% -> 1% of each run, Pallas kernels for 5% -> 5%
where the time goes in v4:
time: 101 us
  blocking collectives  66.2 us (66%)
  Pallas kernels  21.9 us (22%)
  starting transfers between devices  9.61 us (10%)
  other arithmetic  1.61 us (2%)
    all_to_all x1, blocking collectives, body(): lax.all_to_all(blocks.reshape(Z, SLOT // PIECE, PIECE, HD), 'z', 0, 0, ti...  23.3 us
    all_to_all x1, blocking collectives, body(): lax.all_to_all(attended, 'tensor', split_axis=0, concat_axis=1, tiled=True)  21.8 us
    all_to_all x1, blocking collectives, body(): column = lax.all_to_all(column, 'x', 0, 0, tiled=True)  21 us
    pallas_call x1, Pallas kernels, body(): call(far_kernel, jax.ShapeDtypeStruct((TOK, GROUP * HD), half), [VM] * 8,...  15.9 us
    ppermute x1, starting transfers between devices, body(): other = lax.ppermute(column, 'core', [(0, 1), (1, 0)])  8.3 us
    pallas_call x1, Pallas kernels, body(): call(near_kernel, tuple((jax.ShapeDtypeStruct((rows, ROWS), jnp.float32)...  5.41 us
  transfers between devices with their start and end apart: 3, of which 0 were waited for; matrix products, arithmetic and copies ran while one was open for 1% of the time, Pallas kernels for 5%

profile of v4, /device:TPU:3, one launch (start us, length us, event | category | flops | bytes accessed | tf_op | source)
XLA Modules:
  0.0 100.8 jit_solution(41102367880858104)
XLA Ops:
  0.0 0.7 collective-permute-start.1
  0.7 0.7 collective-permute-start
  1.3 0.8 pad_maximum_fusion.1.pair_ref
  2.8 0.7 pad_add_fusion.picks_ref
  3.5 0.0 collective-permute-done.1.passed_values_ref
  3.5 0.0 collective-permute-done.passed_keys_ref
  3.5 0.3 shard_map.55
  3.8 23.3 %all_to_all.29 = bf16[8,12,16,128]{3,2,1,0:T(8,128)(2,1)S(1)} all-to-all(bf16[8,12,16,128]{3,2,1,0:T(8,128)(2,1)S(1)} %bitcast.9), channel_id=1, replica_groups=mesh['z'=8,'x'=4,'core'=2,'tensor'=8] {'z'}, dimensions={0} | all-to-all | bytes 786432 | tf_op jit(solution)/shard_map/all_to_all | solution.py:260
  27.1 0.2 shard_map.56
  27.3 21.0 %all_to_all.30 = bf16[4,96,16,128]{3,2,1,0:T(8,128)(2,1)S(1)} all-to-all(bf16[4,96,16,128]{3,2,1,0:T(8,128)(2,1)S(1)} %bitcast.8), channel_id=1, replica_groups=mesh['z'=8,'x'=4,'core'=2,'tensor'=8] {'x'}, dimensions={0} | all-to-all | bytes 3145728 | tf_op jit(solution)/shard_map/all_to_all | solution.py:266
  48.4 0.0 copy-start
  48.4 0.0 copy-start.1
  48.4 0.0 copy-start.2
  48.4 0.1 pad_maximum_fusion.columns_ref.near_ref
  48.5 8.3 %collective-permute-start.2 = (bf16[6336,128]{1,0:T(8,128)(2,1)S(1)}, bf16[6336,128]{1,0:T(8,128)(2,1)S(1)}, u32[]{:S(2)}, u32[]{:S(2)}) collective-permute-start(bf16[6336,128]{1,0:T(8,128)(2,1)S(1)} %pad_maximum_fusion.columns_ref.near_ref), channel_id=1, source_target_pairs={{0,8},{8,0},{1,9},{9,1},{2,10},{10,2},{3,11},{11,3},{4,12},{12,4},... | collective-permute-start | bytes 4866056 | tf_op jit(solution)/shard_map/ppermute | solution.py:268
  56.8 0.0 copy-done
  56.8 0.0 copy-done.1
  56.8 0.0 copy-done.2
  56.8 5.4 %shard_map.57 = (f32[8,1536]{1,0:T(8,128)S(1)}, f32[136,1536]{1,0:T(8,128)S(1)}, bf16[1536,128]{1,0:T(8,128)(2,1)S(1)}) custom-call(bf16[192,1024]{1,0:T(8,128)(2,1)S(1)} %copy-done.2, bf16[192,128]{1,0:T(8,128)(2,1)S(1)} %copy-done.1, bf16[192,128]{1,0:T(8,128)(2,1)S(1)} %copy-done, bf16[6336,128]{1,0:T(8,128)(2,1)S(1)} %pad_maximum_fusion.columns_ref.near_ref), custom_call_target="tpu_custom_call" | custom-call | flops 2415919104 | bytes 1048576 | tf_op jit(solution)/shard_map/pallas_call | solution.py:271
  62.3 0.0 collective-permute-done.2.columns_ref
  62.3 15.9 %shard_map.58 = bf16[192,1024]{1,0:T(8,128)(2,1)S(1)} custom-call(bf16[1536,128]{1,0:T(8,128)(2,1)S(1)} %get-tuple-element.8.stacked, bf16[192,128]{1,0:T(8,128)(2,1)S(1)} %copy-done.1, bf16[192,128]{1,0:T(8,128)(2,1)S(1)} %collective-permute-done.passed_keys_ref, bf16[192,128]{1,0:T(8,128)(2,1)S(1)} %collective-permute-done.1.passed_values_ref, ...), custom_call_target="tpu_custom_call" | custom-call | flops 2415919104 | bytes 1048576 | tf_op jit(solution)/shard_map/pallas_call | solution.py:279
  78.2 21.8 %all_to_all.31 = bf16[8,24,1024]{2,1,0:T(8,128)(2,1)S(1)} all-to-all(bf16[8,24,1024]{2,1,0:T(8,128)(2,1)S(1)} %bitcast.11), channel_id=1, replica_groups=mesh['z'=8,'x'=4,'core'=2,'tensor'=8] {'tensor'}, dimensions={0} | all-to-all | bytes 786432 | tf_op jit(solution)/shard_map/all_to_all | solution.py:287
  100.0 0.8 copy.7
Async XLA Ops:
  0.0 3.5 %collective-permute-start.1 = (bf16[192,128]{1,0:T(8,128)(2,1)}, bf16[192,128]{1,0:T(8,128)(2,1)S(1)}, u32[]{:S(2)}, u32[]{:S(2)}) collective-permute-start(bf16[192,128]{1,0:T(8,128)(2,1)} %values_ref.1), channel_id=1, source_target_pairs={{0,504},{1,505},{2,506},{3,507},{4,508},{5,509},{6,510},{7,511}} | collective-permute-start | bytes 147464 | tf_op jit(solution)/shard_map/ppermute | solution.py:254
  0.7 2.8 %collective-permute-start = (bf16[192,128]{1,0:T(8,128)(2,1)}, bf16[192,128]{1,0:T(8,128)(2,1)S(1)}, u32[]{:S(2)}, u32[]{:S(2)}) collective-permute-start(bf16[192,128]{1,0:T(8,128)(2,1)} %keys_ref.3), channel_id=1, source_target_pairs={{0,496},{1,497},{2,498},{3,499},{4,500},{5,501},{6,502},{7,503}} | collective-permute-start | bytes 147464 | tf_op jit(solution)/shard_map/ppermute | solution.py:253
  48.4 8.4 %copy-start = (bf16[192,128]{1,0:T(8,128)(2,1)S(1)}, bf16[192,128]{1,0:T(8,128)(2,1)}, u32[]{:S(2)}) copy-start(bf16[192,128]{1,0:T(8,128)(2,1)} %values_ref.1) | copy-start | bytes 147460
  48.4 8.4 %copy-start.1 = (bf16[192,128]{1,0:T(8,128)(2,1)S(1)}, bf16[192,128]{1,0:T(8,128)(2,1)}, u32[]{:S(2)}) copy-start(bf16[192,128]{1,0:T(8,128)(2,1)} %keys_ref.3) | copy-start | bytes 147460
  48.4 8.4 %copy-start.2 = (bf16[192,1024]{1,0:T(8,128)(2,1)S(1)}, bf16[192,1024]{1,0:T(8,128)(2,1)}, u32[]{:S(2)}) copy-start(bf16[192,1024]{1,0:T(8,128)(2,1)} %queries_ref.1) | copy-start | bytes 1179652
  48.5 13.8 %collective-permute-start.2 = (bf16[6336,128]{1,0:T(8,128)(2,1)S(1)}, bf16[6336,128]{1,0:T(8,128)(2,1)S(1)}, u32[]{:S(2)}, u32[]{:S(2)}) collective-permute-start(bf16[6336,128]{1,0:T(8,128)(2,1)S(1)} %pad_maximum_fusion.columns_ref.near_ref), channel_id=1, source_target_pairs={{0,8},{8,0},{1,9},{9,1},{2,10},{10,2},{3,11},{11,3},{4,12},{12,4},... | collective-permute-start | bytes 4866056 | tf_op jit(solution)/shard_map/ppermute | solution.py:268
